TPU v7x, 32 devices: a whole 2x2x4 slice. The times are simulated.
32 devices in a mesh: groups: 2 (over x), hit: 8 (over z, y), query: 2 (over core).
Axes of the slice: x: 2, y: 2, z: 4, core: 2. Of those that a mesh axis runs over, the one named last changes fastest.
Arguments:
- hits: bfloat16 [16384, 512], P(('groups', 'hit', 'query')), parts along dimension 0, may hold values from -24 to 24
- order: int32 [32, 512], P(('groups', 'hit', 'query')), parts along dimension 0, may hold values from 0 to 511, each once within a row
- valid: int32 [16384], P(('groups', 'hit', 'query')), parts along dimension 0, may hold values 0 or 1
- reach: int32 [16384], P(('groups', 'hit', 'query')), parts along dimension 0, may hold values from 128 to 512, as said below
- enc_wq: bfloat16 [512, 512], replicated, may hold values from -3 to 3
- enc_wk: bfloat16 [512, 512], replicated, may hold values from -1 to 1
- enc_wv: bfloat16 [512, 512], replicated, may hold values from -0.25 to 0.25
- enc_wo: bfloat16 [512, 512], replicated, may hold values from -0.25 to 0.25
- enc_gain1: float32 [512], replicated, may hold values from 0.5 to 1.5
- ffn_up: bfloat16 [512, 2048], replicated, may hold values from -0.25 to 0.25
- ffn_down: bfloat16 [2048, 512], replicated, may hold values from -0.125 to 0.125
- enc_gain2: float32 [512], replicated, may hold values from 0.5 to 1.5
- object_queries: bfloat16 [512, 512], P(('groups', 'hit', 'query')), parts along dimension 0, may hold values from -48 to 48
- dec_wq: bfloat16 [512, 512], replicated, may hold values from -8 to 8
- dec_wk: bfloat16 [512, 512], replicated, may hold values from -0.25 to 0.25
- dec_wv: bfloat16 [512, 512], replicated, may hold values from -0.25 to 0.25
- dec_wo: bfloat16 [512, 512], replicated, may hold values from -0.25 to 0.25
- dec_gain: float32 [512], replicated, may hold values from 0.5 to 1.5
- out_proj: bfloat16 [512, 512], replicated, may hold values from -0.25 to 0.25
Outputs:
- encoded: bfloat16 [16384, 512], P(('groups', 'hit', 'query')), parts along dimension 0
- decoded: bfloat16 [512, 512], P(('groups', 'hit', 'query')), parts along dimension 0
There are 2 independent parts, one for each index of `groups`. A program takes and returns all parts, laid end to end along the dimension named above; an argument that names none is the same for every part. Nothing has to cross between parts.
Inputs may be any that keep to these rules, and one draw needn't show every extreme that they name: The first hit of every block of 512 arrival positions has reach 512.
All inputs are finite; a program needn't handle non-finite values. No bound on the sum of `valid` on one device may be relied on, other than what follows from the above.
Results may differ from a plain program's by a relative error of at most 0.035.
Values may be sent and summed in bfloat16 or wider, within the bound.
A program may use at most 192 MiB of HBM per device.

v0:
```python
import math

import jax
import jax.numpy as jnp
from jax import lax
from jax.sharding import PartitionSpec as P

D = 512
HEADS = 8
WINDOW = 512


def padded(cells, sides, width):
    for axis, dim in sides:
        count = lax.axis_size(axis)
        head = lax.slice_in_dim(cells, 0, width, axis=dim)
        tail = lax.slice_in_dim(cells, cells.shape[dim] - width, cells.shape[dim], axis=dim)
        cells = jnp.concatenate(
            [
                lax.ppermute(tail, axis, [(i, (i + 1) % count) for i in range(count)]),
                cells,
                lax.ppermute(head, axis, [((i + 1) % count, i) for i in range(count)]),
            ],
            axis=dim,
        )
    return cells


def joined(value, axis, combine):
    everything = jax.tree.map(lambda part: lax.all_gather(part, axis), value)
    leading = jax.tree.map(lambda part: part[0], everything)

    def lap(k, so_far):
        return combine(so_far, jax.tree.map(lambda part: part[k], everything))

    return lax.fori_loop(1, lax.axis_size(axis), lap, leading)


def project(rows, weight):
    return jnp.dot(rows, weight, preferred_element_type=jnp.float32).astype(jnp.bfloat16)


def rms_norm(values, gain):
    scale = lax.rsqrt(jnp.mean(values * values, axis=-1, keepdims=True) + 1e-05)
    return values * scale * gain


def band_attention(queries, keys, values, key_valid, reach):
    count = queries.shape[0]
    span = keys.shape[0]
    margin = (span - count) // 2
    width = queries.shape[1] // HEADS
    query_heads = queries.reshape(count, HEADS, width)
    key_heads = keys.reshape(span, HEADS, width)
    value_heads = values.reshape(span, HEADS, width)
    scores = jnp.einsum(
        "qhd,khd->hqk", query_heads, key_heads, preferred_element_type=jnp.float32
    ) * (1.0 / math.sqrt(width))
    offset = jnp.arange(span, dtype=jnp.int32)[None, :] - (
        jnp.arange(count, dtype=jnp.int32)[:, None] + margin
    )
    allowed = (jnp.abs(offset) <= reach[:, None]) & ((key_valid[None, :] > 0) | (offset == 0))
    scores = jnp.where(allowed[None], scores, -jnp.inf)
    peak = jnp.max(scores, axis=2, keepdims=True)
    expo = jnp.where(allowed[None], jnp.exp(scores - peak), 0.0)
    probs = (expo / jnp.sum(expo, axis=2, keepdims=True)).astype(jnp.bfloat16)
    context = jnp.einsum("hqk,khd->qhd", probs, value_heads, preferred_element_type=jnp.float32)
    return context.reshape(count, HEADS * width).astype(jnp.bfloat16)


def encoder_tail(context, sorted_hits, enc_wo, enc_gain1, ffn_up, ffn_down, enc_gain2):
    attn_res = jnp.dot(context, enc_wo, preferred_element_type=jnp.float32) + sorted_hits.astype(
        jnp.float32
    )
    middle = rms_norm(attn_res, enc_gain1).astype(jnp.bfloat16)
    hidden = jax.nn.gelu(
        jnp.dot(middle, ffn_up, preferred_element_type=jnp.float32), approximate=True
    ).astype(jnp.bfloat16)
    ffn_res = jnp.dot(hidden, ffn_down, preferred_element_type=jnp.float32) + middle.astype(
        jnp.float32
    )
    return rms_norm(ffn_res, enc_gain2).astype(jnp.bfloat16)


def span_partial(queries, keys, values):
    count = queries.shape[0]
    span = keys.shape[0]
    width = queries.shape[1] // HEADS
    query_heads = queries.reshape(count, HEADS, width)
    key_heads = keys.reshape(span, HEADS, width)
    value_heads = values.reshape(span, HEADS, width)
    scores = jnp.einsum(
        "qhd,khd->qhk", query_heads, key_heads, preferred_element_type=jnp.float32
    ) * (1.0 / math.sqrt(width))
    peak = jnp.max(scores, axis=2)
    expo = jnp.exp(scores - peak[:, :, None])
    total = jnp.sum(expo, axis=2)
    weights = expo.astype(jnp.bfloat16)
    output = jnp.einsum("qhk,khd->qhd", weights, value_heads, preferred_element_type=jnp.float32)
    return (peak, total, output.reshape(count, HEADS * width))


def merge_partials(first, second):
    width = D // HEADS
    peak = jnp.maximum(first[0], second[0])
    left = jnp.exp(first[0] - peak)
    right = jnp.exp(second[0] - peak)
    total = first[1] * left + second[1] * right
    output = first[2] * jnp.repeat(left, width, axis=1) + second[2] * jnp.repeat(
        right, width, axis=1
    )
    return (peak, total, output)


def on_device(
    hits,
    order,
    valid,
    reach,
    enc_wq,
    enc_wk,
    enc_wv,
    enc_wo,
    enc_gain1,
    ffn_up,
    ffn_down,
    enc_gain2,
    object_queries,
    dec_wq,
    dec_wk,
    dec_wv,
    dec_wo,
    dec_gain,
    out_proj,
):
    rows = hits.shape[0]
    place = order[0]
    sorted_hits = hits[place]
    sorted_valid = valid[place].astype(jnp.bfloat16)
    sorted_reach = reach[place]
    queries = project(sorted_hits, enc_wq)
    wide_hits, wide_valid = (
        padded(sorted_hits, ((("hit", "query"), 0),), WINDOW),
        padded(sorted_valid, ((("hit", "query"), 0),), WINDOW),
    )
    wide_keys = project(wide_hits, enc_wk)
    wide_values = project(wide_hits, enc_wv)
    block = 512

    def attend(index):
        start = index * block
        return band_attention(queries, wide_keys, wide_values, wide_valid, sorted_reach)

    context = lax.map(attend, jnp.arange(rows // block, dtype=jnp.int32)).reshape(
        rows, queries.shape[1]
    )
    encoded = encoder_tail(context, sorted_hits, enc_wo, enc_gain1, ffn_up, ffn_down, enc_gain2)
    local_queries = project(object_queries, dec_wq)
    span_keys, span_values = (
        lax.all_gather(project(encoded, dec_wk), "query", axis=0, tiled=True),
        lax.all_gather(project(encoded, dec_wv), "query", axis=0, tiled=True),
    )
    all_queries = lax.all_gather(local_queries, "hit", axis=0, tiled=True)
    count = all_queries.shape[0]
    qblock = 512 if count % 512 == 0 else count

    def partial_block(index):
        return span_partial(all_queries, span_keys, span_values)

    peaks, totals, outputs = lax.map(partial_block, jnp.arange(count // qblock, dtype=jnp.int32))
    width = D // HEADS
    peaks = peaks.reshape(count, HEADS)
    totals = totals.reshape(count, HEADS)
    outputs = outputs.reshape(count, HEADS * width)
    owned = object_queries.shape[0]
    highest, merged_total, merged_out = joined((peaks, totals, outputs), "hit", merge_partials)
    start = lax.axis_index("hit") * owned
    numer = lax.dynamic_slice_in_dim(merged_out, start, owned, 0)
    denom = lax.dynamic_slice_in_dim(merged_total, start, owned, 0)
    cross = (numer / jnp.repeat(denom, width, axis=1)).astype(jnp.bfloat16)
    dec_res = jnp.dot(cross, dec_wo, preferred_element_type=jnp.float32) + object_queries.astype(
        jnp.float32
    )
    normed = rms_norm(dec_res, dec_gain).astype(jnp.bfloat16)
    decoded = jnp.dot(normed, out_proj, preferred_element_type=jnp.float32).astype(jnp.bfloat16)
    return (encoded, decoded)


def solution(mesh):
    in_specs = (
        P(("groups", "hit", "query"), None),
        P(("groups", "hit", "query"), None),
        P(("groups", "hit", "query")),
        P(("groups", "hit", "query")),
        P(),
        P(),
        P(),
        P(),
        P(),
        P(),
        P(),
        P(),
        P(("groups", "hit", "query"), None),
        P(),
        P(),
        P(),
        P(),
        P(),
        P(),
    )
    out_specs = (P(("groups", "hit", "query"), None), P(("groups", "hit", "query"), None))
    return jax.shard_map(
        on_device, mesh=mesh, in_specs=in_specs, out_specs=out_specs, check_vma=False
    )
```

profile of v0, /device:TPU:0, one launch (start us, length us, event | category | flops | bytes accessed | tf_op | source)
XLA Modules:
  0.0 208.1 jit_solution(11262240188574677869)
XLA Ops:
  8.1 3.1 %gather_fusion = bf16[512,512]{1,0:T(8,128)(2,1)S(1)} fusion(bf16[512,512]{1,0:T(8,128)(2,1)} %param.21, s32[1024]{0:T(1024)S(1)} %pad_clamp_fusion), kind=kCustom, calls=%fused_computation | custom fusion | bytes 1050624 | tf_op jit(solution)/shard_map/gather | solution.py:138
  11.7 5.1 %collective-permute-start.1 = (bf16[512,512]{1,0:T(8,128)(2,1)S(1)}, bf16[512,512]{1,0:T(8,128)(2,1)}, u32[]{:S(2)}, u32[]{:S(2)}) collective-permute-start(bf16[512,512]{1,0:T(8,128)(2,1)S(1)} %gather_fusion), channel_id=1, source_target_pairs={{1,0},{2,1},{3,2},{4,3},{5,4},{6,5},{7,6},{8,7},{9,8},{10,9},{11,1... | collective-permute-start | bytes 1572872 | tf_op jit(solution)/shard_map/ppermute | solution.py:22
  16.8 3.5 %gather_fusion.2 = s32[512]{0:T(512)S(1)} fusion(s32[512]{0:T(512)S(1)} %copy-done.1, s32[1024]{0:T(1024)S(1)} %pad_clamp_fusion), kind=kCustom, calls=%fused_computation.2 | custom fusion | bytes 6144 | tf_op jit(solution)/shard_map/gather | solution.py:139
  20.3 4.4 %collective-permute-start.3 = (bf16[512]{0:T(512)(128)(2,1)S(1)}, bf16[512]{0:T(512)(128)(2,1)S(1)}, u32[]{:S(2)}, u32[]{:S(2)}) collective-permute-start(bf16[512]{0:T(512)(128)(2,1)S(1)} %convert_element_type.70), channel_id=1, source_target_pairs={{1,0},{2,1},{3,2},{4,3},{5,4},{6,5},{7,6},{8,7},{9,8},{10,9},{11,1... | collective-permute-start | bytes 3080 | tf_op jit(solution)/shard_map/ppermute | solution.py:22
  24.8 2.3 %convolution_convert_fusion.4 = bf16[512,512]{0,1:T(8,128)(2,1)} fusion(bf16[512,512]{1,0:T(8,128)(2,1)S(1)} %gather_fusion, bf16[512,512]{1,0:T(8,128)(2,1)} %param.25), kind=kOutput, calls=%fused_computation.52 | convolution fusion | flops 268697600 | bytes 1572864 | tf_op jit(solution)/shard_map/dot_general | solution.py:40
  27.3 3.5 %gather_fusion.1 = s32[512]{0:T(512)S(1)} fusion(s32[512]{0:T(512)S(1)} %copy-done.2, s32[1024]{0:T(1024)S(1)} %pad_clamp_fusion), kind=kCustom, calls=%fused_computation.1 | custom fusion | bytes 6144 | tf_op jit(solution)/shard_map/gather | solution.py:140
  30.9 2.5 %fusion.21 = pred[512,1536]{1,0:T(8,128)(4,1)} fusion(s32[512]{0:T(512)S(1)} %gather_fusion.1, s32[512]{0:T(512)S(1)} %iota_add_fusion, pred[1536]{0:T(1024)(128)(4,1)S(1)} %maximum_compare_fusion), kind=kLoop, calls=%fused_computation.39 | loop fusion | flops 4718592 | bytes 792064 | tf_op jit(solution)/shard_map/while/body/eval_jaxpr/and | solution.py:62
  35.6 3.3 %convolution_convert_fusion = bf16[1536,512]{0,1:T(8,128)(2,1)} fusion(bf16[1536,512]{1,0:T(8,128)(2,1)S(1)} %constant_dynamic-update-slice_fusion, bf16[512,512]{1,0:T(8,128)(2,1)} %param.26), kind=kOutput, calls=%fused_computation.41 | convolution fusion | flops 806092800 | bytes 3670016 | tf_op jit(solution)/shard_map/dot_general | solution.py:40
  38.9 2.2 %convolution_convert_fusion.1 = bf16[1536,512]{0,1:T(8,128)(2,1)} fusion(bf16[1536,512]{1,0:T(8,128)(2,1)S(1)} %constant_dynamic-update-slice_fusion, bf16[512,512]{1,0:T(8,128)(2,1)S(1)} %copy-done.11), kind=kOutput, calls=%fused_computation.42 | convolution fusion | flops 806092800 | bytes 3670016 | tf_op jit(solution)/shard_map/dot_general | solution.py:40
  41.1 16.0 %fusion.47 = (f32[8,512]{1,0:T(8,128)S(1)}, f32[8,512,1536]{2,1,0:T(8,128)}) fusion(pred[512,1536]{1,0:T(8,128)(4,1)S(1)} %copy-done.4, bf16[512,8,64]{0,2,1:T(8,128)(2,1)} %bitcast.90, bf16[1536,8,64]{0,2,1:T(8,128)(2,1)} %bitcast.97), kind=kOutput, calls=%fused_computation.87 | convolution fusion | flops 836765184 | bytes 28065792 | tf_op jit(solution)/shard_map/while/body/eval_jaxpr/sub | solution.py:65
  57.1 11.0 %fusion.32 = bf16[8,64,512]{2,1,0:T(8,128)(2,1)S(1)} fusion(bf16[1536,8,64]{0,2,1:T(8,128)(2,1)} %bitcast.96, f32[8,512,1536]{2,1,0:T(8,128)} %get-tuple-element.255, f32[8,512]{1,0:T(8,128)S(1)} %get-tuple-element.254), kind=kOutput, calls=%fused_computation.49 | convolution fusion | flops 818151424 | bytes 27279360 | tf_op jit(solution)/shard_map/while/body/eval_jaxpr/hqk,khd->qhd/dot_general | solution.py:67
  69.6 6.4 %multiply_reduce_fusion = (f32[512]{0:T(512)S(1)}, f32[512,512]{0,1:T(8,128)}) fusion(f32[512]{0:T(512)S(1)} %copy-done.12, f32[512,512]{0,1:T(8,128)} %get-tuple-element.257, f32[512]{0:T(512)S(1)} %add_rsqrt_fusion.1, bf16[2048,512]{1,0:T(8,128)(2,1)S(1)} %copy-done, bf16[512,2048]{1,0:T(8,128)(2,1)} %param.30), kind=kOutput, calls=%fused_computation.57 | convolution fusion | flops 2159541760 | bytes 6297600 | tf_op jit(solution)/shard_map/dot_general | solution.py:79
  77.4 2.5 %convolution_convert_fusion.3 = bf16[512,512]{1,0:T(8,128)(2,1)} fusion(bf16[512,512]{0,1:T(8,128)(2,1)S(1)} %multiply_convert_fusion, bf16[512,512]{1,0:T(8,128)(2,1)} %param.35), kind=kOutput, calls=%fused_computation.51 | convolution fusion | flops 268697600 | bytes 1572864 | tf_op jit(solution)/shard_map/dot_general | solution.py:40
  80.0 2.4 %convolution_convert_fusion.2 = bf16[512,512]{1,0:T(8,128)(2,1)} fusion(bf16[512,512]{0,1:T(8,128)(2,1)S(1)} %multiply_convert_fusion, bf16[512,512]{1,0:T(8,128)(2,1)} %param.36), kind=kOutput, calls=%fused_computation.50 | convolution fusion | flops 268697600 | bytes 1572864 | tf_op jit(solution)/shard_map/dot_general | solution.py:40
  82.6 30.5 %all_gather.19 = bf16[128,512]{1,0:T(8,128)(2,1)S(1)} all-gather(bf16[16,512]{1,0:T(8,128)(2,1)S(1)} %convolution_convert_fusion.6), channel_id=1, replica_groups=mesh['groups'=2,'hit'=8,'query'=2] {'hit'}, dimensions={0}, use_global_device_ids=true | all-gather | bytes 147456 | tf_op jit(solution)/shard_map/all_gather | solution.py:163
  113.3 1.5 copy.38
  114.8 2.8 %bitcast_reduce_fusion = (f32[128,8]{0,1:T(8,128)S(1)}, f32[8,1024,128]{2,1,0:T(8,128)}) fusion(bf16[1024,8,64]{0,2,1:T(8,128)(2,1)S(1)} %bitcast.87, bf16[128,8,64]{0,2,1:T(8,128)(2,1)S(1)} %bitcast.91), kind=kOutput, calls=%fused_computation.32 | convolution fusion | flops 136313856 | bytes 5378048 | tf_op jit(solution)/shard_map/while/body/eval_jaxpr/qhd,khd->qhk/dot_general | solution.py:92
  119.1 3.0 %fusion.23 = f32[8,64,128]{2,1,0:T(8,128)S(1)} fusion(bf16[1024,8,64]{0,2,1:T(8,128)(2,1)S(1)} %bitcast.88, f32[8,1024,128]{2,1,0:T(8,128)} %get-tuple-element.261, f32[128,8]{0,1:T(8,128)S(1)} %get-tuple-element.260), kind=kOutput, calls=%fused_computation.43 | convolution fusion | flops 137363456 | bytes 5509120 | tf_op jit(solution)/shard_map/while/body/eval_jaxpr/qhk,khd->qhd/dot_general | solution.py:99
  123.0 2.0 copy.45
  125.0 2.9 %fusion.19 = f32[128,8]{0,1:T(8,128)S(1)} fusion(f32[8,1024,128]{2,1,0:T(8,128)} %get-tuple-element.261, f32[128,8]{0,1:T(8,128)S(1)} %get-tuple-element.260), kind=kLoop, calls=%fused_computation.35 | loop fusion | flops 3144704 | bytes 4202496 | tf_op jit(solution)/shard_map/while/body/eval_jaxpr/reduce_sum | solution.py:97
  127.9 30.6 %all-gather.1 = f32[1024,8]{0,1:T(8,128)S(1)} all-gather(f32[128,8]{0,1:T(8,128)S(1)} %fusion.19), channel_id=3, replica_groups=mesh['groups'=2,'hit'=8,'query'=2] {'hit'}, dimensions={0}, use_global_device_ids=true | all-gather | bytes 36864 | tf_op jit(solution)/shard_map/all_gather | solution.py:30
  158.5 30.6 %all-gather = f32[1024,8]{0,1:T(8,128)S(1)} all-gather(f32[128,8]{0,1:T(8,128)S(1)} %get-tuple-element.260), channel_id=2, replica_groups=mesh['groups'=2,'hit'=8,'query'=2] {'hit'}, dimensions={0}, use_global_device_ids=true | all-gather | bytes 36864 | tf_op jit(solution)/shard_map/all_gather | solution.py:30
  190.3 8.8 %while.12 = (s32[]{:T(128)}, f32[128,8]{0,1:T(8,128)S(1)}, f32[128,8]{0,1:T(8,128)S(1)}, f32[128,512]{0,1:T(8,128)S(1)}, f32[8,128,8]{1,2,0:T(8,128)S(1)}, /*ind...) while((s32[]{:T(128)}, f32[128,8]{0,1:T(8,128)S(1)}, ...), condition=%wide.region_7.8_spmd, body=%wide.region_6.7_spmd.sunk | while | flops 202757 | bytes 1876119 | solution.py:36
  199.7 1.9 convolution_convert_fusion.5
  (94 shorter events, 19.8 us)
Async XLA Ops:
  7.2 62.4 %copy-start = (bf16[2048,512]{1,0:T(8,128)(2,1)S(1)}, bf16[2048,512]{1,0:T(8,128)(2,1)}, u32[]{:S(2)}) copy-start(bf16[2048,512]{1,0:T(8,128)(2,1)} %param.31) | copy-start | bytes 6291460
  7.2 9.6 %copy-start.1 = (s32[512]{0:T(512)S(1)}, s32[512]{0:T(512)}, u32[]{:S(2)}) copy-start(s32[512]{0:T(512)} %param.23) | copy-start | bytes 6148
  7.2 106.1 %all-gather.6.cloned.1.call-start = ((), (), s32[]{:S(2)}) async-start(), calls=%async_computation | async-start | bytes 1572864 | tf_op jit(solution)/shard_map/all_gather | solution.py:160
  8.1 19.2 %copy-start.2 = (s32[512]{0:T(512)S(1)}, s32[512]{0:T(512)}, u32[]{:S(2)}) copy-start(s32[512]{0:T(512)} %param.24) | copy-start | bytes 6148
  11.2 22.2 %collective-permute-start = (bf16[512,512]{1,0:T(8,128)(2,1)S(1)}, bf16[512,512]{1,0:T(8,128)(2,1)}, u32[]{:S(2)}, u32[]{:S(2)}) collective-permute-start(bf16[512,512]{1,0:T(8,128)(2,1)S(1)} %gather_fusion), channel_id=1, source_target_pairs={{0,1},{1,2},{2,3},{3,4},{4,5},{5,6},{6,7},{7,8},{8,9},{9,10},{10,1... | collective-permute-start | bytes 1572872 | tf_op jit(solution)/shard_map/ppermute | solution.py:20
  11.7 22.8 %collective-permute-start.1 = (bf16[512,512]{1,0:T(8,128)(2,1)S(1)}, bf16[512,512]{1,0:T(8,128)(2,1)}, u32[]{:S(2)}, u32[]{:S(2)}) collective-permute-start(bf16[512,512]{1,0:T(8,128)(2,1)S(1)} %gather_fusion), channel_id=1, source_target_pairs={{1,0},{2,1},{3,2},{4,3},{5,4},{6,5},{7,6},{8,7},{9,8},{10,9},{11,1... | collective-permute-start | bytes 1572872 | tf_op jit(solution)/shard_map/ppermute | solution.py:22
  20.3 10.5 %collective-permute-start.2 = (bf16[512]{0:T(512)(128)(2,1)S(1)}, bf16[512]{0:T(512)(128)(2,1)S(1)}, u32[]{:S(2)}, u32[]{:S(2)}) collective-permute-start(bf16[512]{0:T(512)(128)(2,1)S(1)} %convert_element_type.70), channel_id=1, source_target_pairs={{0,1},{1,2},{2,3},{3,4},{4,5},{5,6},{6,7},{7,8},{8,9},{9,10},{10,1... | collective-permute-start | bytes 3080 | tf_op jit(solution)/shard_map/ppermute | solution.py:20
  20.3 10.5 %collective-permute-start.3 = (bf16[512]{0:T(512)(128)(2,1)S(1)}, bf16[512]{0:T(512)(128)(2,1)S(1)}, u32[]{:S(2)}, u32[]{:S(2)}) collective-permute-start(bf16[512]{0:T(512)(128)(2,1)S(1)} %convert_element_type.70), channel_id=1, source_target_pairs={{1,0},{2,1},{3,2},{4,3},{5,4},{6,5},{7,6},{8,7},{9,8},{10,9},{11,1... | collective-permute-start | bytes 3080 | tf_op jit(solution)/shard_map/ppermute | solution.py:22
  30.8 8.1 %copy-start.11 = (bf16[512,512]{1,0:T(8,128)(2,1)S(1)}, bf16[512,512]{1,0:T(8,128)(2,1)}, u32[]{:S(2)}) copy-start(bf16[512,512]{1,0:T(8,128)(2,1)} %param.27) | copy-start | bytes 1572868
  35.6 5.5 %copy-start.4 = (pred[512,1536]{1,0:T(8,128)(4,1)S(1)}, pred[512,1536]{1,0:T(8,128)(4,1)}, u32[]{:S(2)}) copy-start(pred[512,1536]{1,0:T(8,128)(4,1)} %fusion.21) | copy-start | bytes 2359300
  57.1 11.0 %copy-start.7 = (bf16[512,512]{1,0:T(8,128)(2,1)S(1)}, bf16[512,512]{1,0:T(8,128)(2,1)}, u32[]{:S(2)}) copy-start(bf16[512,512]{1,0:T(8,128)(2,1)} %param.28) | copy-start | bytes 1572868
  57.1 12.5 %copy-start.12 = (f32[512]{0:T(512)S(1)}, f32[512]{0:T(512)}, u32[]{:S(2)}) copy-start(f32[512]{0:T(512)} %param.29) | copy-start | bytes 6148
  69.6 6.4 %copy-start.9 = (f32[512]{0:T(512)S(1)}, f32[512]{0:T(512)}, u32[]{:S(2)}) copy-start(f32[512]{0:T(512)} %param.32) | copy-start | bytes 6148
  75.9 6.5 %copy-start.6 = (bf16[512,512]{1,0:T(8,128)(2,1)S(1)}, bf16[512,512]{1,0:T(8,128)(2,1)}, u32[]{:S(2)}) copy-start(bf16[512,512]{1,0:T(8,128)(2,1)} %param.34) | copy-start | bytes 1572868
  76.0 6.5 %copy-start.8 = (bf16[16,512]{1,0:T(8,128)(2,1)S(1)}, bf16[16,512]{1,0:T(8,128)(2,1)}, u32[]{:S(2)}) copy-start(bf16[16,512]{1,0:T(8,128)(2,1)} %param.33) | copy-start | bytes 49156
  77.4 35.9 %copy-start.3 = (bf16[512,512]{0,1:T(8,128)(2,1)}, bf16[512,512]{0,1:T(8,128)(2,1)S(1)}, u32[]{:S(2)}) copy-start(bf16[512,512]{0,1:T(8,128)(2,1)S(1)} %multiply_convert_fusion) | copy-start | bytes 1572868
  79.9 37.6 %all-gather.8.cloned.1.call-start = ((), (), s32[]{:S(2)}) async-start(), calls=%async_computation.1 | async-start | bytes 1572864 | tf_op jit(solution)/shard_map/all_gather | solution.py:161
  82.4 106.8 %all-gather.10.cloned.1.call-start = ((), (), s32[]{:S(2)}) async-start(), calls=%async_computation.2 | async-start | bytes 2359296 | tf_op jit(solution)/shard_map/all_gather | solution.py:30
  190.2 9.1 %copy-start.5 = (bf16[512,512]{1,0:T(8,128)(2,1)S(1)}, bf16[512,512]{1,0:T(8,128)(2,1)}, u32[]{:S(2)}) copy-start(bf16[512,512]{1,0:T(8,128)(2,1)} %param.37) | copy-start | bytes 1572868
  190.2 9.4 %copy-start.10 = (f32[512]{0:T(512)S(1)}, f32[512]{0:T(512)}, u32[]{:S(2)}) copy-start(f32[512]{0:T(512)} %param.38) | copy-start | bytes 6148
Sparse Core Ops, SparseCore 0:
  80.1 6.6 all-gather.5
  88.3 10.1 all-gather.7
  123.1 47.3 all-gather.9
where the time goes:
time: 209 us; the launch traced here: 208 us
  blocking collectives  91.7 us (44%)
  matrix products  55.6 us (27%)
  local copies, waits for them, and re-layouts  27.4 us (13%)
  between operations  14.1 us (7%)
  starting transfers between devices  10.2 us (5%)
  other arithmetic  8.66 us (4%)
    all_gather x2, blocking collectives, joined(): everything = jax.tree.map(lambda part: lax.all_gather(part, axis), value)  61.2 us
    all_gather x1, blocking collectives, on_device(): all_queries = lax.all_gather(local_queries, 'hit', axis=0, tiled=True)  30.5 us
    sub x1, matrix products, band_attention(): expo = jnp.where(allowed[None], jnp.exp(scores - peak), 0.0)  16 us
    dot_general x6, matrix products, project(): jnp.dot(rows, weight, preferred_element_type=jnp.float32)  12.8 us
    dot_general x1, matrix products, band_attention(): jnp.einsum('hqk,khd->qhd', probs, value_heads, preferred_element_type=jnp...  11 us
    ppermute x2, starting transfers between devices, padded(): lax.ppermute(head, axis, [((i + 1) % count, i) for i in range(count)])  9.49 us
    dynamic_slice x14, local copies, waits for them, and re-layouts, lap(): return combine(so_far, jax.tree.map(lambda part: part[k], everything))  7.72 us
    dot_general x1, matrix products, encoder_tail(): jnp.dot(hidden, ffn_down, preferred_element_type=jnp.float32)  6.36 us
  transfers between devices with their start and end apart: 7, of which 0 were waited for; matrix products, arithmetic and copies ran while one was open for 12% of the time, Pallas kernels for 0%

commit v1 on v0

v1 whole, which is shorter than its diff:
```python
import functools
import math

import jax
import jax.numpy as jnp
from jax import lax
from jax.experimental import pallas as pl
from jax.experimental.pallas import tpu as pltpu
from jax.sharding import PartitionSpec as P

HEADS = 8
LANES = 128
TAIL = 16
MESH = pl.DeviceIdType.MESH
BF16 = jnp.bfloat16
F32 = jnp.float32
FAR = -1e30
NT = (((1,), (1,)), ((), ()))


def dot(a, b):
    return jnp.dot(a, b, preferred_element_type=F32)


def dot_nt(a, b):
    return lax.dot_general(a, b, NT, preferred_element_type=F32)


def rms_norm(values, gain):
    scale = lax.rsqrt(jnp.mean(values * values, axis=-1, keepdims=True) + 1e-05)
    return values * scale * gain


def gelu(x):
    inner = math.sqrt(2.0 / math.pi) * (x + 0.044715 * (x * x * x))
    return 0.5 * x * (1.0 + jnp.tanh(inner))


def kernel(
    n_hit,
    n_query,
    order_ref,
    valid_ref,
    reach_ref,
    gain1_ref,
    gain2_ref,
    dgain_ref,
    objq_ref,
    hits_hbm,
    wq_hbm,
    wk_hbm,
    wv_hbm,
    dwq_hbm,
    wo_hbm,
    up_hbm,
    down_hbm,
    dwk_hbm,
    dwv_hbm,
    dwo_hbm,
    out_hbm,
    enc_hbm,
    dec_ref,
    hits_s,
    wq_s,
    wk_s,
    wv_s,
    dwq_s,
    wo_s,
    up_s,
    down_s,
    dwk_s,
    dwv_s,
    dwo_s,
    out_s,
    ext_s,
    halo_s,
    q_s,
    k_s,
    v_s,
    bias_s,
    acc_s,
    mx_s,
    ctx_s,
    ffn_s,
    enc_s,
    dk_s,
    dv_s,
    qall_s,
    o_s,
    lse_s,
    pair_s,
    pairin_s,
    msg_s,
    msgin_s,
    load_sem,
    halo_send,
    halo_recv,
    dq_send,
    dq_recv,
    pair_send,
    pair_recv,
    msg_send,
    msg_recv,
    enc_sem,
):
    group = lax.axis_index("groups")
    hit = lax.axis_index("hit")
    core = lax.axis_index("query")
    count = n_hit * n_query
    me = hit * n_query + core
    n, width = hits_s.shape
    half = n // 2
    pairs = width // LANES
    head_width = width // HEADS
    owned = objq_ref.shape[0]
    part = n_hit * owned
    factor = math.log2(math.e) / math.sqrt(head_width)

    loads = [
        pltpu.make_async_copy(source, target, load_sem.at[i])
        for i, (source, target) in enumerate(
            (
                (hits_hbm, hits_s),
                (dwq_hbm, dwq_s),
                (wq_hbm, wq_s),
                (wk_hbm, wk_s),
                (wv_hbm, wv_s),
                (wo_hbm, wo_s),
                (up_hbm, up_s),
                (down_hbm, down_s),
                (dwk_hbm, dwk_s),
                (dwv_hbm, dwv_s),
                (dwo_hbm, dwo_s),
                (out_hbm, out_s),
            )
        )
    ]
    for load in loads:
        load.start()

    def device(block):
        return (group, lax.div(block, n_query), lax.rem(block, n_query))

    barrier = pltpu.get_barrier_semaphore()

    def greet(d, carry):
        pl.semaphore_signal(
            barrier, inc=1, device_id=device(lax.rem(me + d, count)), device_id_type=MESH
        )
        return carry

    lax.fori_loop(1, count, greet, 0)

    order_rows = jnp.broadcast_to(order_ref[...].astype(F32), (LANES, n))
    order_col = jnp.transpose(order_rows)[:, :1].astype(jnp.int32)
    hot = lax.broadcasted_iota(jnp.int32, (n, n), 1) == order_col
    onehot = jnp.where(hot, 1.0, 0.0)
    reach_col = jnp.sum(onehot * reach_ref[...].astype(F32), axis=1, keepdims=True)
    onehot = onehot.astype(BF16)
    valid_rows = jnp.broadcast_to(valid_ref[...].astype(F32), (TAIL, n)).astype(BF16)
    sorted_valid = dot_nt(valid_rows, onehot)
    ext_s[pl.ds(n, TAIL), :] = sorted_valid.astype(BF16)
    loads[0].wait()
    ext_s[pl.ds(0, n), :] = dot(onehot, hits_s[...]).astype(BF16)

    pl.semaphore_wait(barrier, count - 1)

    right = lax.rem(me + 1, count)
    left = lax.rem(me + count - 1, count)
    halo = []
    for side, target in ((0, right), (1, left)):
        copy = pltpu.make_async_remote_copy(
            src_ref=ext_s,
            dst_ref=halo_s.at[side],
            send_sem=halo_send.at[side],
            recv_sem=halo_recv.at[side],
            device_id=device(target),
            device_id_type=MESH,
        )
        copy.start()
        halo.append(copy)

    loads[1].wait()
    my_slot = core * n_hit + hit
    qall_s[my_slot] = (dot(objq_ref[...], dwq_s[...]) * factor).astype(BF16)

    def dq_copy(d):
        peer = lax.rem(me + d, count)
        return pltpu.make_async_remote_copy(
            src_ref=qall_s.at[my_slot],
            dst_ref=qall_s.at[my_slot],
            send_sem=dq_send.at[d],
            recv_sem=dq_recv.at[my_slot],
            device_id=device(peer),
            device_id_type=MESH,
        )

    def dq_start(d, carry):
        dq_copy(d).start()
        return carry

    lax.fori_loop(1, count, dq_start, 0)

    for load in loads[2:5]:
        load.wait()
    own = pl.ds(n, n)
    rows = ext_s[pl.ds(0, n), :]
    q_s[...] = (dot(rows, wq_s[...]) * factor).astype(BF16)
    k_s[own, :] = dot(rows, wk_s[...]).astype(BF16)
    v_s[own, :] = dot(rows, wv_s[...]).astype(BF16)

    def bias_of(place, valid_row):
        offset = (
            lax.broadcasted_iota(jnp.int32, (n, n), 1)
            - lax.broadcasted_iota(jnp.int32, (n, n), 0)
            + (place - 1) * n
        )
        far = jnp.abs(offset).astype(F32) > reach_col
        gone = (valid_row < 0.5) & (offset != 0)
        bias_s[:, pl.ds(place * n, n)] = jnp.where(far | gone, FAR, 0.0)

    bias_of(1, sorted_valid[:1, :])

    lane = lax.broadcasted_iota(jnp.int32, (1, LANES), 1)
    first = jnp.where(lane < head_width, 1.0, 0.0)
    keep = (first.astype(BF16), (1.0 - first).astype(BF16))

    def own_pair(p, carry):
        cols = pl.ds(pl.multiple_of(p * LANES, LANES), LANES)
        qp, kp, vp = q_s[:, cols], k_s[own, cols], v_s[own, cols]
        for h in range(2):
            s = dot_nt(qp * keep[h], kp) + bias_s[:, own]
            m = jnp.max(s, axis=1, keepdims=True)
            weights = jnp.exp2(s - m).astype(BF16)
            acc_s[p, h] = dot(weights, vp * keep[h] + keep[1 - h])
            mx_s[p, h] = jnp.broadcast_to(m, (n, LANES))
        return carry

    lax.fori_loop(0, pairs, own_pair, 0)

    for side in range(2):
        halo[side].wait_recv()
        there = pl.ds(2 * side * n, n)
        rows = halo_s[side, pl.ds(0, n), :]
        k_s[there, :] = dot(rows, wk_s[...]).astype(BF16)
        v_s[there, :] = dot(rows, wv_s[...]).astype(BF16)
        bias_of(2 * side, halo_s[side, pl.ds(n, TAIL), :].astype(F32)[:1, :])

    def split_heads(o0, o1):
        front = lane < head_width
        return (
            jnp.where(front, o0, o1),
            pltpu.roll(jnp.where(front, o1, o0), head_width, 1),
        )

    def wide_pair(p, carry):
        cols = pl.ds(pl.multiple_of(p * LANES, LANES), LANES)
        for tile, spans in (
            (0, (pl.ds(0, n), pl.ds(2 * n, half))),
            (1, (pl.ds(half, half), pl.ds(2 * n, n))),
        ):
            here = pl.ds(tile * half, half)
            qp = q_s[here, cols]
            outs = []
            for h in range(2):
                qh = qp * keep[h]
                scores = [dot_nt(qh, k_s[span, cols]) + bias_s[here, span] for span in spans]
                before = mx_s[p, h, here, :]
                m = before[:, :1]
                for s in scores:
                    m = jnp.maximum(m, jnp.max(s, axis=1, keepdims=True))
                out = acc_s[p, h, here, :] * jnp.exp2(before - m)
                for s, span in zip(scores, spans):
                    out += dot(
                        jnp.exp2(s - m).astype(BF16), v_s[span, cols] * keep[h] + keep[1 - h]
                    )
                outs.append(out)
            value, total = split_heads(*outs)
            ctx_s[here, cols] = (value / total).astype(BF16)
        return carry

    lax.fori_loop(0, pairs, wide_pair, 0)

    for load in loads[5:8]:
        load.wait()
    middle = rms_norm(
        dot(ctx_s[...], wo_s[...]) + ext_s[pl.ds(0, n), :].astype(F32), gain1_ref[...]
    ).astype(BF16)
    ffn_s[...] = middle.astype(F32)
    hidden_width = up_s.shape[1]
    step = 512

    for c in range(hidden_width // step):
        hidden = gelu(dot(middle, up_s[:, pl.ds(c * step, step)])).astype(BF16)
        ffn_s[...] += dot(hidden, down_s[pl.ds(c * step, step), :])
    encoded = rms_norm(ffn_s[...], gain2_ref[...]).astype(BF16)
    enc_s[...] = encoded
    enc_copy = pltpu.make_async_copy(enc_s, enc_hbm, enc_sem)
    enc_copy.start()

    loads[8].wait()
    loads[9].wait()
    dk_s[...] = dot(encoded, dwk_s[...]).astype(BF16)
    dv_s[...] = dot(encoded, dwv_s[...]).astype(BF16)

    def dq_wait(d, carry):
        peer = lax.rem(me + d, count)
        slot = lax.rem(peer, n_query) * n_hit + lax.div(peer, n_query)
        pltpu.make_async_remote_copy(
            src_ref=qall_s.at[slot],
            dst_ref=qall_s.at[slot],
            send_sem=dq_send.at[d],
            recv_sem=dq_recv.at[slot],
            device_id=device(peer),
            device_id_type=MESH,
        ).wait_recv()
        return carry

    lax.fori_loop(1, count, dq_wait, 0)

    def partial(which):
        slots = pl.ds(which * n_hit, n_hit)

        for p in range(pairs):
            cols = pl.ds(p * LANES, LANES)
            qp = qall_s[slots, :, cols].reshape(part, LANES)
            kp, vp = dk_s[:, cols], dv_s[:, cols]
            outs, tops = [], []
            for h in range(2):
                s = dot_nt(qp * keep[h], kp)
                m = jnp.max(s, axis=1, keepdims=True)
                outs.append(dot(jnp.exp2(s - m).astype(BF16), vp * keep[h] + keep[1 - h]))
                tops.append(m)
            value, total = split_heads(*outs)
            o_s[:, cols] = value / total
            lse_s[:, cols] = jnp.where(lane < head_width, tops[0], tops[1]) + jnp.log2(total)

    column = lax.broadcasted_iota(jnp.int32, (width, LANES), 0)
    slot_of = lax.broadcasted_iota(jnp.int32, (width, LANES), 1)

    def packed(lse):
        total = jnp.zeros((lse.shape[0], LANES), F32)
        rest = lse
        for k in range(3):
            term = rest.astype(BF16)
            rest = rest - term.astype(F32)
            pick = jnp.where(column == (slot_of - k * HEADS) * head_width, 1.0, 0.0)
            total += dot(term, pick.astype(BF16))
        return total.astype(BF16)

    spread_row = lax.broadcasted_iota(jnp.int32, (LANES, width), 0)
    spread_col = lax.broadcasted_iota(jnp.int32, (LANES, width), 1)
    spread = jnp.zeros((LANES, width), F32)
    for k in range(3):
        low = (spread_row - k * HEADS) * head_width
        spread += jnp.where((spread_col >= low) & (spread_col < low + head_width), 1.0, 0.0)
    spread = spread.astype(BF16)

    partial(1 - core)
    pair_s[:, pl.ds(0, width)] = o_s[...].astype(BF16)
    pair_s[:, pl.ds(width, LANES)] = packed(lse_s[...])
    pair_copy = pltpu.make_async_remote_copy(
        src_ref=pair_s,
        dst_ref=pairin_s,
        send_sem=pair_send,
        recv_sem=pair_recv,
        device_id=(group, hit, 1 - core),
        device_id_type=MESH,
    )
    pair_copy.start()
    partial(core)
    pair_copy.wait_recv()
    lse_a, lse_b = lse_s[...], dot(pairin_s[:, pl.ds(width, LANES)], spread)
    top = jnp.maximum(lse_a, lse_b)
    wa, wb = jnp.exp2(lse_a - top), jnp.exp2(lse_b - top)
    total = wa + wb
    merged = (wa * o_s[...] + wb * pairin_s[:, pl.ds(0, width)].astype(F32)) / total
    msg_s[:, :, pl.ds(0, width)] = merged.astype(BF16).reshape(n_hit, owned, width)
    msg_s[:, :, pl.ds(width, LANES)] = packed(top + jnp.log2(total)).reshape(
        n_hit, owned, LANES
    )

    def msg_copy(d):
        peer = lax.rem(hit + d, n_hit)
        return pltpu.make_async_remote_copy(
            src_ref=msg_s.at[peer],
            dst_ref=msgin_s.at[hit],
            send_sem=msg_send.at[d],
            recv_sem=msg_recv.at[hit],
            device_id=(group, peer, core),
            device_id_type=MESH,
        )

    def msg_start(d, carry):
        msg_copy(d).start()
        return carry

    lax.fori_loop(1, n_hit, msg_start, 0)
    msgin_s[hit] = msg_s[hit]
    loads[10].wait()
    loads[11].wait()

    def msg_wait(d, carry):
        peer = lax.rem(hit + d, n_hit)
        pltpu.make_async_remote_copy(
            src_ref=msg_s.at[peer],
            dst_ref=msgin_s.at[peer],
            send_sem=msg_send.at[d],
            recv_sem=msg_recv.at[peer],
            device_id=(group, peer, core),
            device_id_type=MESH,
        ).wait_recv()
        return carry

    lax.fori_loop(1, n_hit, msg_wait, 0)
    values = msgin_s[:, :, pl.ds(0, width)].astype(F32)
    lse = dot(msgin_s[:, :, pl.ds(width, LANES)].reshape(part, LANES), spread)
    lse = lse.reshape(n_hit, owned, width)
    weights = jnp.exp2(lse - jnp.max(lse, axis=0, keepdims=True))
    cross = jnp.sum(weights * values, axis=0) / jnp.sum(weights, axis=0)
    res = dot(cross.astype(BF16), dwo_s[...]) + objq_ref[...].astype(F32)
    normed = rms_norm(res, dgain_ref[...]).astype(BF16)
    dec_ref[...] = dot(normed, out_s[...]).astype(BF16)

    for copy in halo:
        copy.wait_send()

    def dq_sent(d, carry):
        dq_copy(d).wait_send()
        return carry

    lax.fori_loop(1, count, dq_sent, 0)
    pair_copy.wait_send()

    def msg_sent(d, carry):
        msg_copy(d).wait_send()
        return carry

    lax.fori_loop(1, n_hit, msg_sent, 0)
    enc_copy.wait()


def on_device(
    n_hit,
    n_query,
    hits,
    order,
    valid,
    reach,
    enc_wq,
    enc_wk,
    enc_wv,
    enc_wo,
    enc_gain1,
    ffn_up,
    ffn_down,
    enc_gain2,
    object_queries,
    dec_wq,
    dec_wk,
    dec_wv,
    dec_wo,
    dec_gain,
    out_proj,
):
    n, width = hits.shape
    owned = object_queries.shape[0]
    hidden = ffn_up.shape[1]
    count = n_hit * n_query
    part = n_hit * owned
    pairs = width // LANES
    vmem = pl.BlockSpec(memory_space=pltpu.VMEM)
    anywhere = pl.BlockSpec(memory_space=pl.ANY)
    square = pltpu.VMEM((width, width), BF16)
    dma = pltpu.SemaphoreType.DMA
    return pl.pallas_call(
        functools.partial(kernel, n_hit, n_query),
        out_shape=(
            jax.ShapeDtypeStruct((n, width), BF16),
            jax.ShapeDtypeStruct((owned, width), BF16),
        ),
        in_specs=[vmem] * 7 + [anywhere] * 12,
        out_specs=(anywhere, vmem),
        scratch_shapes=[
            pltpu.VMEM((n, width), BF16),
            square,
            square,
            square,
            square,
            square,
            pltpu.VMEM((width, hidden), BF16),
            pltpu.VMEM((hidden, width), BF16),
            square,
            square,
            square,
            square,
            pltpu.VMEM((n + TAIL, width), BF16),
            pltpu.VMEM((2, n + TAIL, width), BF16),
            pltpu.VMEM((n, width), BF16),
            pltpu.VMEM((3 * n, width), BF16),
            pltpu.VMEM((3 * n, width), BF16),
            pltpu.VMEM((n, 3 * n), F32),
            pltpu.VMEM((pairs, 2, n, LANES), F32),
            pltpu.VMEM((pairs, 2, n, LANES), F32),
            pltpu.VMEM((n, width), BF16),
            pltpu.VMEM((n, width), F32),
            pltpu.VMEM((n, width), BF16),
            pltpu.VMEM((n, width), BF16),
            pltpu.VMEM((n, width), BF16),
            pltpu.VMEM((count, owned, width), BF16),
            pltpu.VMEM((part, width), F32),
            pltpu.VMEM((part, width), F32),
            pltpu.VMEM((part, width + LANES), BF16),
            pltpu.VMEM((part, width + LANES), BF16),
            pltpu.VMEM((n_hit, owned, width + LANES), BF16),
            pltpu.VMEM((n_hit, owned, width + LANES), BF16),
            dma((12,)),
            dma((2,)),
            dma((2,)),
            dma((count,)),
            dma((count,)),
            dma,
            dma,
            dma((n_hit,)),
            dma((n_hit,)),
            dma,
        ],
        compiler_params=pltpu.CompilerParams(
            collective_id=0, has_side_effects=True, vmem_limit_bytes=56 * 1024 * 1024
        ),
        name="track",
    )(
        order,
        valid.reshape(1, n),
        reach.reshape(1, n),
        enc_gain1.reshape(1, width),
        enc_gain2.reshape(1, width),
        dec_gain.reshape(1, width),
        object_queries,
        hits,
        enc_wq,
        enc_wk,
        enc_wv,
        dec_wq,
        enc_wo,
        ffn_up,
        ffn_down,
        dec_wk,
        dec_wv,
        dec_wo,
        out_proj,
    )


def solution(mesh):
    split = P(("groups", "hit", "query"), None)
    flat = P(("groups", "hit", "query"))
    in_specs = (split, split, flat, flat) + (P(),) * 8 + (split,) + (P(),) * 6
    return jax.shard_map(
        functools.partial(on_device, mesh.shape["hit"], mesh.shape["query"]),
        mesh=mesh,
        in_specs=in_specs,
        out_specs=(split, split),
        check_vma=False,
    )
```

time: 209 us -> 54.1 us (0.26)
  blocking collectives: 91.7 us -> 0 us
  matrix products: 55.6 us -> 0 us
  Pallas kernels: 0 us -> 50 us
  local copies, waits for them, and re-layouts: 27.4 us -> 3.19 us
  between operations: 14.1 us -> 0.65 us
  starting transfers between devices: 10.2 us -> 0 us
  other arithmetic: 8.66 us -> 0 us
    all_gather x3 -> x0, blocking collectives: 91.7 us -> none  [the longest x2 61.2 us: joined(): everything = jax.tree.map(lambda part: lax.all_gather(part, axis), value)]
    pallas_call x0 -> x1, Pallas kernels: none -> 50 us  [on_device(): pl.pallas_call(functools.partial(kernel, n_hit, n_query), out_shape=(jax....]
    dot_general x13 -> x0, matrix products: 39.7 us -> none  [the longest x6 12.8 us: project(): jnp.dot(rows, weight, preferred_element_type=jnp.float32)]
    sub x1 -> x0, matrix products: 16 us -> none  [band_attention(): expo = jnp.where(allowed[None], jnp.exp(scores - peak), 0.0)]
    gather x4 -> x0, local copies, waits for them, and re-layouts: 10.3 us -> none  [the longest x1 3.49 us: on_device(): sorted_reach = reach[place]]
    ppermute x4 -> x0, starting transfers between devices: 10.1 us -> none  [the longest x2 9.49 us: padded(): lax.ppermute(head, axis, [((i + 1) % count, i) for i in range(count)])]
    dynamic_slice x15 -> x0, local copies, waits for them, and re-layouts: 7.8 us -> none  [the longest x14 7.72 us: lap(): return combine(so_far, jax.tree.map(lambda part: part[k], everything))]
    all_gather x3 -> x0, local copies, waits for them, and re-layouts: 3.09 us -> none  [the longest x1 1.49 us: on_device(): lax.all_gather(project(encoded, dec_wk), 'query', axis=0, tiled=True)]
  transfers between devices with their start and end apart: 7 -> 0, of which waited for: 0 -> 0; matrix products, arithmetic and copies ran while one was open for 12% -> 0% of each run, Pallas kernels for 0% -> 0%
where the time goes in v1:
time: 54.1 us; the launch traced here: 53.8 us
  Pallas kernels  50 us (92%)
  local copies, waits for them, and re-layouts  3.19 us (6%)
  between operations  0.65 us (1%)
    pallas_call x1, Pallas kernels, on_device(): pl.pallas_call(functools.partial(kernel, n_hit, n_query), out_shape=(jax....  50 us
    unnamed x2, local copies, waits for them, and re-layouts  3.19 us

profile of v1, /device:TPU:0, one launch (start us, length us, event | category | flops | bytes accessed | tf_op | source)
XLA Modules:
  0.0 53.8 jit_solution(4263600552292947935)
XLA Ops:
  0.6 50.0 %track.1 = (bf16[512,512]{1,0:T(8,128)(2,1)}, bf16[16,512]{1,0:T(8,128)(2,1)}) custom-call(s32[1,512]{1,0:T(1,128)} %order_ref.1, s32[1,512]{1,0:T(1,128)} %bitcast.5, s32[1,512]{1,0:T(1,128)} %bitcast.6, f32[1,512]{1,0:T(1,128)} %bitcast.7, f32[1,512]{1,0:T(1,128)} %bitcast.8, f32[1,512]{1,0:T(1,128)} %bitcast.9, bf16[16,512]{1,0:T(8,128)(2,1)} %objq_ref.1, ...), custom_call_target="tpu_custom_call" | custom-call | tf_op jit(solution)/shard_map/track/pallas_call | solution.py:476
  50.6 1.9 %copy.23 = bf16[512,512]{1,0:T(8,128)(2,1)} copy(bf16[512,512]{1,0:T(8,128)(2,1)} %get-tuple-element.4) | data formatting | bytes 1048576
  52.5 1.3 %copy.24 = bf16[16,512]{1,0:T(8,128)(2,1)} copy(bf16[16,512]{1,0:T(8,128)(2,1)} %get-tuple-element.5) | data formatting | bytes 32768

commit v2 on v1

--- a/solution.py
+++ b/solution.py
@@ -159,26 +159,44 @@
     onehot = onehot.astype(BF16)
     valid_rows = jnp.broadcast_to(valid_ref[...].astype(F32), (TAIL, n)).astype(BF16)
     sorted_valid = dot_nt(valid_rows, onehot)
-    ext_s[pl.ds(n, TAIL), :] = sorted_valid.astype(BF16)
+    ext_s[pl.ds(0, TAIL), :] = sorted_valid.astype(BF16)
+    ext_s[pl.ds(n + TAIL, TAIL), :] = sorted_valid.astype(BF16)
     loads[0].wait()
-    ext_s[pl.ds(0, n), :] = dot(onehot, hits_s[...]).astype(BF16)
+    ext_s[pl.ds(TAIL, n), :] = dot(onehot, hits_s[...]).astype(BF16)
 
     pl.semaphore_wait(barrier, count - 1)
 
-    right = lax.rem(me + 1, count)
-    left = lax.rem(me + count - 1, count)
-    halo = []
-    for side, target in ((0, right), (1, left)):
-        copy = pltpu.make_async_remote_copy(
+    near_side, far_side = 1 - core, core
+    far_block = lax.rem(me + count - 1 + 2 * core, count)
+    piece = half + TAIL
+
+    def near_copy(side):
+        return pltpu.make_async_remote_copy(
             src_ref=ext_s,
             dst_ref=halo_s.at[side],
-            send_sem=halo_send.at[side],
-            recv_sem=halo_recv.at[side],
-            device_id=device(target),
+            send_sem=halo_send.at[0],
+            recv_sem=halo_recv.at[0],
+            device_id=(group, hit, 1 - core),
             device_id_type=MESH,
         )
-        copy.start()
-        halo.append(copy)
+
+    def far_copy(side, k):
+        if k == 0:
+            span = pl.ds(pl.multiple_of((1 - side) * piece, TAIL), piece)
+        else:
+            span = pl.ds(pl.multiple_of(TAIL + side * half, TAIL), half)
+        return pltpu.make_async_remote_copy(
+            src_ref=ext_s.at[span],
+            dst_ref=halo_s.at[side, span],
+            send_sem=halo_send.at[1 + k],
+            recv_sem=halo_recv.at[1 + k],
+            device_id=device(far_block),
+            device_id_type=MESH,
+        )
+
+    far_copy(1 - core, 0).start()
+    far_copy(1 - core, 1).start()
+    near_copy(core).start()
 
     loads[1].wait()
     my_slot = core * n_hit + hit
@@ -204,22 +222,22 @@
     for load in loads[2:5]:
         load.wait()
     own = pl.ds(n, n)
-    rows = ext_s[pl.ds(0, n), :]
+    rows = ext_s[pl.ds(TAIL, n), :]
     q_s[...] = (dot(rows, wq_s[...]) * factor).astype(BF16)
     k_s[own, :] = dot(rows, wk_s[...]).astype(BF16)
     v_s[own, :] = dot(rows, wv_s[...]).astype(BF16)
 
-    def bias_of(place, valid_row):
+    def bias_of(start, size, valid_row):
         offset = (
-            lax.broadcasted_iota(jnp.int32, (n, n), 1)
-            - lax.broadcasted_iota(jnp.int32, (n, n), 0)
-            + (place - 1) * n
+            lax.broadcasted_iota(jnp.int32, (n, size), 1)
+            - lax.broadcasted_iota(jnp.int32, (n, size), 0)
+            + (start - n)
         )
         far = jnp.abs(offset).astype(F32) > reach_col
         gone = (valid_row < 0.5) & (offset != 0)
-        bias_s[:, pl.ds(place * n, n)] = jnp.where(far | gone, FAR, 0.0)
-
-    bias_of(1, sorted_valid[:1, :])
+        bias_s[:, pl.ds(start, size)] = jnp.where(far | gone, FAR, 0.0)
+
+    bias_of(n, n, sorted_valid[:1, :])
 
     lane = lax.broadcasted_iota(jnp.int32, (1, LANES), 1)
     first = jnp.where(lane < head_width, 1.0, 0.0)
@@ -236,15 +254,7 @@
             mx_s[p, h] = jnp.broadcast_to(m, (n, LANES))
         return carry
 
-    lax.fori_loop(0, pairs, own_pair, 0)
-
-    for side in range(2):
-        halo[side].wait_recv()
-        there = pl.ds(2 * side * n, n)
-        rows = halo_s[side, pl.ds(0, n), :]
-        k_s[there, :] = dot(rows, wk_s[...]).astype(BF16)
-        v_s[there, :] = dot(rows, wv_s[...]).astype(BF16)
-        bias_of(2 * side, halo_s[side, pl.ds(n, TAIL), :].astype(F32)[:1, :])
+    lax.fori_loop(0, pairs, own_pair, 0, unroll=2)
 
     def split_heads(o0, o1):
         front = lane < head_width
@@ -253,38 +263,82 @@
             pltpu.roll(jnp.where(front, o1, o0), head_width, 1),
         )
 
-    def wide_pair(p, carry):
+    def place(side, start, size):
+        there = pl.multiple_of(2 * side * n + start, half)
+        rows = halo_s[side, pl.ds(pl.multiple_of(TAIL + start, TAIL), size), :]
+        k_s[pl.ds(there, size), :] = dot(rows, wk_s[...]).astype(BF16)
+        v_s[pl.ds(there, size), :] = dot(rows, wv_s[...]).astype(BF16)
+        valid_at = pl.multiple_of((1 - side) * (n + TAIL), TAIL)
+        valid_row = halo_s[side, pl.ds(valid_at, TAIL), pl.ds(pl.multiple_of(start, half), size)]
+        bias_of(there, size, valid_row.astype(F32)[:1, :])
+
+    def extended(p, h, here, span):
         cols = pl.ds(pl.multiple_of(p * LANES, LANES), LANES)
-        for tile, spans in (
-            (0, (pl.ds(0, n), pl.ds(2 * n, half))),
-            (1, (pl.ds(half, half), pl.ds(2 * n, n))),
-        ):
-            here = pl.ds(tile * half, half)
-            qp = q_s[here, cols]
-            outs = []
+        s = dot_nt(q_s[here, cols] * keep[h], k_s[span, cols]) + bias_s[here, span]
+        before = mx_s[p, h, here, :]
+        m = jnp.maximum(before[:, :1], jnp.max(s, axis=1, keepdims=True))
+        out = acc_s[p, h, here, :] * jnp.exp2(before - m)
+        out += dot(jnp.exp2(s - m).astype(BF16), v_s[span, cols] * keep[h] + keep[1 - h])
+        return out, m
+
+    def tile(base, k, size=half):
+        return pl.ds(pl.multiple_of(base + k * half, half), size)
+
+    def carry_on(p, jobs):
+        for here, span in jobs:
             for h in range(2):
-                qh = qp * keep[h]
-                scores = [dot_nt(qh, k_s[span, cols]) + bias_s[here, span] for span in spans]
-                before = mx_s[p, h, here, :]
-                m = before[:, :1]
-                for s in scores:
-                    m = jnp.maximum(m, jnp.max(s, axis=1, keepdims=True))
-                out = acc_s[p, h, here, :] * jnp.exp2(before - m)
-                for s, span in zip(scores, spans):
-                    out += dot(
-                        jnp.exp2(s - m).astype(BF16), v_s[span, cols] * keep[h] + keep[1 - h]
-                    )
-                outs.append(out)
-            value, total = split_heads(*outs)
-            ctx_s[here, cols] = (value / total).astype(BF16)
-        return carry
-
-    lax.fori_loop(0, pairs, wide_pair, 0)
+                out, m = extended(p, h, here, span)
+                acc_s[p, h, here, :] = out
+                mx_s[p, h, here, :] = jnp.broadcast_to(m, out.shape)
+
+    near_copy(near_side).wait_recv()
+    place(near_side, 0, n)
+    near_base, near_t = 2 * near_side * n, 1 - near_side
+
+    def near_pair(p, carry):
+        carry_on(
+            p,
+            (
+                (tile(0, near_t), tile(near_base, near_t)),
+                (tile(0, 1 - near_t), tile(near_base, 0, n)),
+            ),
+        )
+        return carry
+
+    lax.fori_loop(0, pairs, near_pair, 0, unroll=2)
+
+    far_base, far_t = 2 * far_side * n, 1 - far_side
+    far_copy(far_side, 0).wait_recv()
+    place(far_side, far_t * half, half)
+
+    def far_pair(p, carry):
+        carry_on(p, ((pl.ds(0, n), tile(far_base, far_t)),))
+        return carry
+
+    lax.fori_loop(0, pairs, far_pair, 0, unroll=2)
+
+    far_copy(far_side, 1).wait_recv()
+    place(far_side, (1 - far_t) * half, half)
+
+    def last_pair(p, carry):
+        cols = pl.ds(pl.multiple_of(p * LANES, LANES), LANES)
+        here = tile(0, far_t)
+        value, total = split_heads(acc_s[p, 0, here, :], acc_s[p, 1, here, :])
+        ctx_s[here, cols] = (value / total).astype(BF16)
+        here = tile(0, 1 - far_t)
+        span = tile(far_base, 1 - far_t)
+        value, total = split_heads(
+            extended(p, 0, here, span)[0], extended(p, 1, here, span)[0]
+        )
+        ctx_s[here, cols] = (value / total).astype(BF16)
+        return carry
+
+    lax.fori_loop(0, pairs, last_pair, 0, unroll=2)
 
     for load in loads[5:8]:
         load.wait()
     middle = rms_norm(
-        dot(ctx_s[...], wo_s[...]) + ext_s[pl.ds(0, n), :].astype(F32), gain1_ref[...]
+        dot(ctx_s[...], wo_s[...]) + ext_s[pl.ds(TAIL, n), :].astype(F32), gain1_ref[...]
     ).astype(BF16)
     ffn_s[...] = middle.astype(F32)
     hidden_width = up_s.shape[1]
@@ -422,8 +476,9 @@
     normed = rms_norm(res, dgain_ref[...]).astype(BF16)
     dec_ref[...] = dot(normed, out_s[...]).astype(BF16)
 
-    for copy in halo:
-        copy.wait_send()
+    far_copy(1 - core, 0).wait_send()
+    far_copy(1 - core, 1).wait_send()
+    near_copy(core).wait_send()
 
     def dq_sent(d, carry):
         dq_copy(d).wait_send()
@@ -438,6 +493,11 @@
 
     lax.fori_loop(1, n_hit, msg_sent, 0)
     enc_copy.wait()
+
+
+def hand_over(enc_in, dec_in, enc_out, dec_out):
+    enc_out[...] = enc_in[...]
+    dec_out[...] = dec_in[...]
 
 
 def on_device(
@@ -473,7 +533,7 @@
     anywhere = pl.BlockSpec(memory_space=pl.ANY)
     square = pltpu.VMEM((width, width), BF16)
     dma = pltpu.SemaphoreType.DMA
-    return pl.pallas_call(
+    raw = pl.pallas_call(
         functools.partial(kernel, n_hit, n_query),
         out_shape=(
             jax.ShapeDtypeStruct((n, width), BF16),
@@ -494,8 +554,8 @@
             square,
             square,
             square,
-            pltpu.VMEM((n + TAIL, width), BF16),
-            pltpu.VMEM((2, n + TAIL, width), BF16),
+            pltpu.VMEM((n + 2 * TAIL, width), BF16),
+            pltpu.VMEM((2, n + 2 * TAIL, width), BF16),
             pltpu.VMEM((n, width), BF16),
             pltpu.VMEM((3 * n, width), BF16),
             pltpu.VMEM((3 * n, width), BF16),
@@ -515,8 +575,8 @@
             pltpu.VMEM((n_hit, owned, width + LANES), BF16),
             pltpu.VMEM((n_hit, owned, width + LANES), BF16),
             dma((12,)),
-            dma((2,)),
-            dma((2,)),
+            dma((3,)),
+            dma((3,)),
             dma((count,)),
             dma((count,)),
             dma,
@@ -550,6 +610,13 @@
         dec_wo,
         out_proj,
     )
+    return pl.pallas_call(
+        hand_over,
+        out_shape=tuple(jax.ShapeDtypeStruct(r.shape, r.dtype) for r in raw),
+        in_specs=[vmem] * 2,
+        out_specs=(vmem, vmem),
+        name="hand_over",
+    )(*raw)
 
 
 def solution(mesh):

time: 54.1 us -> 46.9 us (0.87)
  Pallas kernels: 50 us -> 46.1 us
  local copies, waits for them, and re-layouts: 3.19 us -> 0 us
    pallas_call x1, Pallas kernels: 50 us -> 44.2 us  [on_device(): pl.pallas_call(functools.partial(kernel, n_hit, n_query), out_shape=(jax....]
    unnamed x2 -> x0, local copies, waits for them, and re-layouts: 3.19 us -> none
    pallas_call x0 -> x1, Pallas kernels: none -> 1.87 us  [on_device(): pl.pallas_call(hand_over, out_shape=tuple((jax.ShapeDtypeStruct(r.shape,...]
where the time goes in v2:
time: 46.9 us; the launch traced here: 46.7 us
  Pallas kernels  46.1 us (98%)
  between operations  0.65 us (1%)
    pallas_call x1, Pallas kernels, on_device(): pl.pallas_call(functools.partial(kernel, n_hit, n_query), out_shape=(jax....  44.2 us
    pallas_call x1, Pallas kernels, on_device(): pl.pallas_call(hand_over, out_shape=tuple((jax.ShapeDtypeStruct(r.shape,...  1.87 us

profile of v2, /device:TPU:0, one launch (start us, length us, event | category | flops | bytes accessed | tf_op | source)
XLA Modules:
  0.0 46.7 jit_solution(17504841599215811350)
XLA Ops:
  0.6 44.2 %track.1 = (bf16[512,512]{1,0:T(8,128)(2,1)}, bf16[16,512]{1,0:T(8,128)(2,1)}) custom-call(s32[1,512]{1,0:T(1,128)} %order_ref.1, s32[1,512]{1,0:T(1,128)} %bitcast.5, s32[1,512]{1,0:T(1,128)} %bitcast.6, f32[1,512]{1,0:T(1,128)} %bitcast.7, f32[1,512]{1,0:T(1,128)} %bitcast.8, f32[1,512]{1,0:T(1,128)} %bitcast.9, bf16[16,512]{1,0:T(8,128)(2,1)} %objq_ref.1, ...), custom_call_target="tpu_custom_call" | custom-call | tf_op jit(solution)/shard_map/track/pallas_call | solution.py:536
  44.9 1.9 %hand_over.1 = (bf16[512,512]{1,0:T(8,128)(2,1)}, bf16[16,512]{1,0:T(8,128)(2,1)}) custom-call(bf16[512,512]{1,0:T(8,128)(2,1)} %get-tuple-element.4.enc_in, bf16[16,512]{1,0:T(8,128)(2,1)} %get-tuple-element.5.dec_in), custom_call_target="tpu_custom_call" | custom-call | tf_op jit(solution)/shard_map/hand_over/pallas_call | solution.py:613
